TPU v7x, 128 devices: a whole 4x4x4 slice. The times are simulated.
128 devices in a mesh: batch: 4 (over y), tp: 4 (over z), ep: 8 (over x, core).
Axes of the slice: x: 4, y: 4, z: 4, core: 2. Of those that a mesh axis runs over, the one named last changes fastest.
Arguments:
- states: bfloat16 [32, 512, 2048], P(('batch', 'ep')), may hold values from -30 to 30
- input_gain: float32 [2048], replicated, may hold values from 0.1 to 1.9
- query_weight: bfloat16 [2048, 4096], P(None, 'tp'), may hold values from -0.125 to 0.125
- key_weight: bfloat16 [2048, 512], P(None, 'tp'), may hold values from -0.125 to 0.125
- value_weight: bfloat16 [2048, 512], P(None, 'tp'), may hold values from -0.125 to 0.125
- query_gain: float32 [128], replicated, may hold values from 1 to 2.5
- key_gain: float32 [128], replicated, may hold values from 0.4 to 1.6
- output_weight: bfloat16 [4096, 2048], P('tp'), may hold values from -0.09375 to 0.09375
- mixture_gain: float32 [2048], replicated, may hold values from 0.1 to 1.9
- expert_gate: bfloat16 [128, 2048, 768], P(('batch', 'tp', 'ep')), may hold values from -0.125 to 0.125
- expert_up: bfloat16 [128, 2048, 768], P(('batch', 'tp', 'ep')), may hold values from -0.125 to 0.125
- expert_down: bfloat16 [128, 768, 2048], P(('batch', 'tp', 'ep')), may hold values from -0.21875 to 0.21875
- gate_scale: float32 [128, 768], P(('batch', 'tp', 'ep')), may hold values from 0.5 to 2
- up_scale: float32 [128, 768], P(('batch', 'tp', 'ep')), may hold values from 0.5 to 2
- down_scale: float32 [128, 2048], P(('batch', 'tp', 'ep')), may hold values from 0.5 to 2
- expert_index: int32 [32, 512, 8], P(('batch', 'ep'), 'tp'), may hold values from 0 to 127, as said below
- expert_slot: int32 [32, 512, 8], P(('batch', 'ep'), 'tp'), may hold values from 0 to 9, as said below
- route_weight: float32 [32, 512, 8], P(('batch', 'ep'), 'tp'), may hold values from 0.05 to 0.35
Outputs:
- layer_output: bfloat16 [32, 512, 2048], P(('batch', 'ep'), 'tp')
Inputs may be any that keep to these rules, and one draw needn't show every extreme that they name: `expert_index`: the 8 experts of a token differ. A pair's positions fall into aligned blocks of 128; within one block no expert is named by more than 10 tokens, in every block some expert is named by exactly 10 tokens, and one expert is named by exactly 10 tokens in every block. `expert_slot`: within one aligned block of 128 positions of a pair, the tokens that name the same expert carry different slots.
All inputs are finite; a program needn't handle non-finite values.
Results may differ from a plain program's by a relative error of at most 0.012.
Values may be sent and summed in bfloat16 or wider, within the bound.
A program may use at most 128 MiB of HBM per device.

v0:
```python
import math

import jax
import jax.numpy as jnp
import numpy as np
from jax import lax
from jax.experimental import pallas as pl
from jax.experimental.pallas import tpu as pltpu
from jax.sharding import PartitionSpec as P


def rms_scale(values, scaling):
    mean_square = jnp.mean(values * values, axis=-1, keepdims=True)
    return values * lax.rsqrt(mean_square + 1e-06) * scaling


def rotate(values, positions):
    half_dim = values.shape[-1] // 2
    freq_index = jnp.arange(half_dim, dtype=jnp.float32)
    frequency = jnp.exp(-(2.0 * freq_index / values.shape[-1]) * math.log(1000000.0))
    angles = positions[:, None] * frequency[None, :]
    cosine_table = jnp.cos(angles)[:, None, :]
    sine_table = jnp.sin(angles)[:, None, :]
    first_half = values[..., :half_dim]
    second = values[..., half_dim:]
    return jnp.concatenate(
        [
            first_half * cosine_table - second * sine_table,
            second * cosine_table + first_half * sine_table,
        ],
        axis=-1,
    )


def attend(pair_states, input_gain, query_weight, key_weight, value_weight, query_gain, key_gain):
    pair_count, length, features = pair_states.shape
    head_size = query_gain.shape[0]
    normed = (
        rms_scale(pair_states.astype(jnp.float32), input_gain)
        .astype(jnp.bfloat16)
        .reshape(pair_count * length, features)
    )
    positions = jnp.arange(length, dtype=jnp.float32)
    queries = jnp.dot(normed, query_weight, preferred_element_type=jnp.float32).reshape(
        pair_count, length, -1, head_size
    )
    queries = rotate(rms_scale(queries, query_gain), positions).astype(jnp.bfloat16)
    key_vectors = jnp.dot(normed, key_weight, preferred_element_type=jnp.float32).reshape(
        pair_count, length, -1, head_size
    )
    key_vectors = rotate(rms_scale(key_vectors, key_gain), positions).astype(jnp.bfloat16)
    value_vectors = (
        jnp.dot(normed, value_weight, preferred_element_type=jnp.float32)
        .astype(jnp.bfloat16)
        .reshape(pair_count, length, -1, head_size)
    )
    kv_count = key_vectors.shape[2]
    group_size = queries.shape[2] // kv_count
    queries = queries.reshape(pair_count, length, kv_count, group_size, head_size)
    scores = jnp.einsum(
        "pshgd,pthd->phgst", queries, key_vectors, preferred_element_type=jnp.float32
    ) * (1.0 / math.sqrt(head_size))
    weights = jnp.exp(scores)
    probabilities = (weights / jnp.sum(weights, axis=-1, keepdims=True)).astype(jnp.bfloat16)
    context = jnp.einsum(
        "phgst,pthd->pshgd", probabilities, value_vectors, preferred_element_type=jnp.float32
    )
    return context.astype(jnp.bfloat16).reshape(pair_count, length, -1)


MESH = pl.DeviceIdType.MESH
CUTS = ((0, 768), (768, 640), (1408, 640))
AXES = (("z", "x", "y"), ("x", "y", "z"), ("y", "z", "x"))
BLOCK = 128
CAP = 10
UNIT = 8 * CAP
GROUP = 4 * UNIT


def position():
    ep = lax.axis_index("ep")
    return {
        "y": lax.axis_index("batch"),
        "z": lax.axis_index("tp"),
        "x": ep // 2,
        "c": ep % 2,
    }


def moved(me, axis, value):
    there = dict(me)
    there[axis] = value
    return (there["y"], there["z"], there["x"] * 2 + there["c"])


def step(value, distance):
    return lax.rem(value + distance, 4)


def rows_at(index, size):
    return pl.ds(pl.multiple_of(index * size, size), size)


def landed(ref, sem):
    pltpu.make_async_copy(ref, ref, sem).wait()


def push(src, dst, send_sem, recv_sem, device):
    pltpu.make_async_remote_copy(
        src_ref=src,
        dst_ref=dst,
        send_sem=send_sem,
        recv_sem=recv_sem,
        device_id=device,
        device_id_type=MESH,
    ).start()


def routes(me, chunk, weighted, table, select):
    _, axis_b, axis_c = AXES[chunk]

    def body(j, carry):
        there = dict(me)
        there[axis_b] = j // 4
        there[axis_c] = j % 4
        expert = (there["y"] * 4 + there["z"]) * 8 + there["x"] * 2 + there["c"]
        first = expert.astype(jnp.float32) * CAP
        for k in range(8):
            top = (CAP * k) // 8 * 8
            slot = lax.broadcasted_iota(jnp.int32, (16, BLOCK), 0) + (top - CAP * k)
            wanted = jnp.where(
                (slot >= 0) & (slot < CAP), slot.astype(jnp.float32) + first, -1.0
            )
            found = jnp.zeros((16, BLOCK), jnp.float32)
            for q in range(8):
                column = table[chunk, k, q : q + 1, :]
                value = table[chunk, k, 8 + q : 9 + q, :] if weighted else 1.0
                found = jnp.where(wanted == column, value, found)
            parts = [found]
            if top:
                parts.insert(0, jnp.zeros((top, BLOCK), jnp.float32))
            if top < UNIT - 16:
                parts.append(jnp.zeros((UNIT - 16 - top, BLOCK), jnp.float32))
            select[rows_at(j, UNIT), k * BLOCK : (k + 1) * BLOCK] = jnp.concatenate(
                parts, axis=0
            ).astype(jnp.bfloat16)
        return carry

    lax.fori_loop(0, 16, body, 0)


def mixture_kernel(
    rows_ref,
    hidden_ref,
    table_ref,
    swap_ref,
    gate_scale,
    up_scale,
    down_scale,
    gate_hbm,
    up_hbm,
    down_hbm,
    out_ref,
    gate_w,
    up_w,
    down_w,
    table,
    *scratch,
):
    per = 8
    G, O, M, X, N, R, S, H = [scratch[3 * i : 3 * i + 3] for i in range(per)]
    T = scratch[24:27]
    (
        w_sem,
        p_send,
        p_recv,
        pc_send,
        g_send,
        g_recv,
        gc_send,
        b_send,
        b_recv,
        c_send,
        c_recv,
        rc_send,
        rc_recv,
        rb_send,
        rb_recv,
        k_send,
        k_recv,
        t_send,
        t_recv,
    ) = scratch[27:]
    me = position()
    core = me["c"]
    other = (me["y"], me["z"], me["x"] * 2 + (1 - core))

    barrier = pltpu.get_barrier_semaphore()
    for axis in "zxy":
        for d in (1, 2, 3):
            pl.semaphore_signal(
                barrier,
                inc=1,
                device_id=moved(me, axis, step(me[axis], d)),
                device_id_type=MESH,
            )
    pl.semaphore_signal(barrier, inc=1, device_id=other, device_id_type=MESH)
    pl.semaphore_wait(barrier, 10)

    def block_of(a):
        return core * 4 + a

    for chunk, (start, size) in enumerate(CUTS):
        axis = AXES[chunk][0]
        a = me[axis]
        k = block_of(a)
        pltpu.make_async_copy(table_ref, table.at[chunk, k], p_recv.at[chunk, k]).start()
        for d in (1, 3, 2):
            push(
                table_ref,
                table.at[chunk, k],
                p_send.at[chunk, d],
                p_recv.at[chunk, k],
                moved(me, axis, step(a, d)),
            )
    for chunk, (start, size) in enumerate(CUTS):
        axis = AXES[chunk][0]
        a = me[axis]
        k = block_of(a)
        mine = rows_ref.at[:, pl.ds(start, size)]
        place = G[chunk].at[rows_at(k, BLOCK)]
        pltpu.make_async_copy(mine, place, g_recv.at[chunk, k]).start()
        for d in (1, 3, 2):
            push(
                mine,
                place,
                g_send.at[chunk, d],
                g_recv.at[chunk, k],
                moved(me, axis, step(a, d)),
            )
    for n, (src, dst) in enumerate(((gate_hbm, gate_w), (up_hbm, up_w), (down_hbm, down_w))):
        pltpu.make_async_copy(src, dst, w_sem.at[n]).start()
    for d in (0, 1, 3, 2):
        for chunk in range(3):
            k = block_of(step(me[AXES[chunk][0]], d))
            landed(table.at[chunk, k], p_recv.at[chunk, k])
            push(
                table.at[chunk, k],
                table.at[chunk, k],
                pc_send.at[chunk, d],
                p_recv.at[chunk, k],
                other,
            )
    for chunk in range(3):
        for a in range(4):
            k = (1 - core) * 4 + a
            landed(table.at[chunk, k], p_recv.at[chunk, k])
        routes(me, chunk, False, table, S[chunk])
    for d in (0, 1, 3, 2):
        for chunk in range(3):
            k = block_of(step(me[AXES[chunk][0]], d))
            place = G[chunk].at[rows_at(k, BLOCK)]
            landed(place, g_recv.at[chunk, k])
            push(place, place, gc_send.at[chunk, d], g_recv.at[chunk, k], other)

    for chunk in range(3):
        axis = AXES[chunk][1]
        for a in range(4):
            k = (1 - core) * 4 + a
            landed(G[chunk].at[rows_at(k, BLOCK)], g_recv.at[chunk, k])

        def pick(n, carry, chunk=chunk, axis=axis):
            mine = me[axis]
            beta = step(mine, n + 1)
            O[chunk][beta] = jnp.dot(
                S[chunk][rows_at(beta, GROUP), :],
                G[chunk][...],
                preferred_element_type=jnp.float32,
            ).astype(jnp.bfloat16)

            @pl.when(n < 3)
            def _():
                push(
                    O[chunk].at[beta],
                    M[chunk].at[mine],
                    b_send.at[chunk, n],
                    b_recv.at[chunk, mine],
                    moved(me, axis, beta),
                )

            @pl.when(n == 3)
            def _():
                pltpu.make_async_copy(
                    O[chunk].at[beta], M[chunk].at[mine], b_recv.at[chunk, mine]
                ).start()

            return carry

        lax.fori_loop(0, 4, pick, 0)

    def place_of(chunk, beta, gamma):
        return (beta, gamma) if chunk == 1 else (gamma, beta)

    for d in (0, 1, 3, 2):
        for chunk in range(3):
            _, axis_b, axis_c = AXES[chunk]
            beta = step(me[axis_b], d)
            mine = me[axis_c]
            landed(M[chunk].at[beta], b_recv.at[chunk, beta])
            i, j = place_of(chunk, beta, mine)
            for e in (1, 3, 2, 0):
                gamma = step(mine, e)
                src = M[chunk].at[beta, rows_at(gamma, UNIT)]
                dst = X[chunk].at[i, rows_at(j, UNIT)]
                if e:
                    push(
                        src,
                        dst,
                        c_send.at[chunk, d * 4 + e],
                        c_recv.at[chunk, i * 4 + j],
                        moved(me, axis_c, gamma),
                    )
                else:
                    pltpu.make_async_copy(src, dst, c_recv.at[chunk, i * 4 + j]).start()

    for chunk, (start, size) in enumerate(CUTS):
        for d in (1, 2, 3):
            landed(table_ref, p_send.at[chunk, d])
            landed(rows_ref.at[:, pl.ds(start, size)], g_send.at[chunk, d])
        for d in range(4):
            landed(table_ref, pc_send.at[chunk, d])
            landed(G[chunk].at[pl.ds(0, BLOCK)], gc_send.at[chunk, d])
        for n in range(3):
            landed(O[chunk].at[0], b_send.at[chunk, n])
    for n, dst in enumerate((gate_w, up_w, down_w)):
        landed(dst, w_sem.at[n])
    for chunk in (2, 1, 0):
        for i in range(4):
            for j in range(4):
                landed(X[chunk].at[i, pl.ds(j * UNIT, UNIT)], c_recv.at[chunk, i * 4 + j])
        for d in range(4):
            for e in (1, 2, 3):
                landed(X[chunk].at[0, pl.ds(0, UNIT)], c_send.at[chunk, d * 4 + e])

    swap = swap_ref[...]

    def regroup(i, carry):
        turned = jnp.dot(swap, X[2][i], preferred_element_type=jnp.float32).astype(jnp.bfloat16)
        for n in range(4):
            M[2][n, rows_at(i, UNIT), :] = turned[n * UNIT : (n + 1) * UNIT]
        return carry

    lax.fori_loop(0, 4, regroup, 0)

    def expert(n, carry):
        y = step(me["y"], n + 1)
        first = X[0][y]
        second = jnp.dot(swap, X[1][y], preferred_element_type=jnp.float32).astype(jnp.bfloat16)
        third = M[2][y]

        def project(w):
            total = None
            for part, (start, size) in zip((first, second, third), CUTS):
                term = jnp.dot(
                    part, w[start : start + size, :], preferred_element_type=jnp.float32
                )
                total = term if total is None else total + term
            return total

        gate = project(gate_w) * gate_scale[...]
        up = project(up_w) * up_scale[...]
        activated = (gate / (1.0 + jnp.exp(-gate)) * up).astype(jnp.bfloat16)

        def finish(chunk):
            start, size = CUTS[chunk]
            return (
                jnp.dot(
                    activated, down_w[:, start : start + size], preferred_element_type=jnp.float32
                )
                * down_scale[:, start : start + size]
            ).astype(jnp.bfloat16)

        O[0][y] = finish(0)

        @pl.when(n < 3)
        def _():
            push(
                O[0].at[y],
                N[0].at[me["y"]],
                rc_send.at[0, n],
                rc_recv.at[0, me["y"]],
                moved(me, "y", y),
            )

        @pl.when(n == 3)
        def _():
            pltpu.make_async_copy(O[0].at[y], N[0].at[me["y"]], rc_recv.at[0, me["y"]]).start()

        O[1][y] = jnp.dot(swap, finish(1), preferred_element_type=jnp.float32).astype(jnp.bfloat16)
        for e in (1, 3, 2, 0):
            z = step(me["z"], e)
            src = O[1].at[y, rows_at(z, UNIT)]
            dst = N[1].at[me["z"], rows_at(y, UNIT)]
            if e:
                push(
                    src,
                    dst,
                    rc_send.at[1, n * 4 + e],
                    rc_recv.at[1, me["z"] * 4 + y],
                    moved(me, "z", z),
                )
            else:
                pltpu.make_async_copy(src, dst, rc_recv.at[1, me["z"] * 4 + y]).start()
        X[2][y] = finish(2)
        return carry

    lax.fori_loop(0, 4, expert, 0)

    def restore(n, carry):
        mine = me["x"]
        x = step(mine, n + 1)
        parts = jnp.concatenate([X[2][y, rows_at(x, UNIT), :] for y in range(4)], axis=0)
        O[2][x] = jnp.dot(swap, parts, preferred_element_type=jnp.float32).astype(jnp.bfloat16)

        @pl.when(n < 3)
        def _():
            push(
                O[2].at[x],
                N[2].at[mine],
                rc_send.at[2, n],
                rc_recv.at[2, mine],
                moved(me, "x", x),
            )

        @pl.when(n == 3)
        def _():
            pltpu.make_async_copy(O[2].at[x], N[2].at[mine], rc_recv.at[2, mine]).start()

        return carry

    lax.fori_loop(0, 4, restore, 0)

    for chunk in range(3):
        routes(me, chunk, True, table, S[chunk])
    for d in (0, 1, 3, 2):
        for chunk in range(3):
            _, axis_b, axis_c = AXES[chunk]
            gamma = step(me[axis_c], d)
            mine = me[axis_b]
            if chunk == 1:
                for n in range(4):
                    landed(N[1].at[gamma, pl.ds(n * UNIT, UNIT)], rc_recv.at[1, gamma * 4 + n])
            else:
                landed(N[chunk].at[gamma], rc_recv.at[chunk, gamma])
            for e in (1, 3, 2, 0):
                beta = step(mine, e)
                src = N[chunk].at[gamma, rows_at(beta, UNIT)]
                dst = R[chunk].at[rows_at(mine * 4 + gamma, UNIT)]
                if e:
                    push(
                        src,
                        dst,
                        rb_send.at[chunk, d * 4 + e],
                        rb_recv.at[chunk, mine * 4 + gamma],
                        moved(me, axis_b, beta),
                    )
                else:
                    pltpu.make_async_copy(src, dst, rb_recv.at[chunk, mine * 4 + gamma]).start()

    def total(chunk, half):
        return lax.dot_general(
            S[chunk][:, rows_at(half, 512)],
            R[chunk][...],
            (((0,), (0,)), ((), ())),
            preferred_element_type=jnp.float32,
        )

    for chunk in range(3):
        for j in range(16):
            landed(R[chunk].at[pl.ds(j * UNIT, UNIT)], rb_recv.at[chunk, j])
        G[chunk][512:, :] = total(chunk, 1 - core).astype(jnp.bfloat16)
        push(G[chunk].at[pl.ds(512, 512)], H[chunk], k_send.at[chunk], k_recv.at[chunk], other)
    for chunk in range(3):
        axis = AXES[chunk][0]
        mine = me[axis]
        own = total(chunk, core)
        landed(H[chunk], k_recv.at[chunk])
        G[chunk][:512, :] = (own + H[chunk][...].astype(jnp.float32)).astype(jnp.bfloat16)
        for d in (1, 3, 2):
            a = step(mine, d)
            push(
                G[chunk].at[rows_at(a, BLOCK)],
                T[chunk].at[d - 1],
                t_send.at[chunk, d - 1],
                t_recv.at[chunk, d - 1],
                moved(me, axis, a),
            )
    for chunk, (start, size) in enumerate(CUTS):
        mine = me[AXES[chunk][0]]
        result = hidden_ref[:, start : start + size] + G[chunk][rows_at(mine, BLOCK), :].astype(
            jnp.float32
        )
        for d in range(3):
            landed(T[chunk].at[d], t_recv.at[chunk, d])
            result = result + T[chunk][d].astype(jnp.float32)
        out_ref[:, start : start + size] = result.astype(jnp.bfloat16)

    for chunk in range(3):
        for n in range(3):
            if chunk != 1:
                landed(O[chunk].at[0], rc_send.at[chunk, n])
            landed(T[chunk].at[0], t_send.at[chunk, n])
        if chunk == 1:
            for n in range(4):
                for e in (1, 2, 3):
                    landed(O[1].at[0, pl.ds(0, UNIT)], rc_send.at[1, n * 4 + e])
        landed(H[chunk], k_send.at[chunk])
        for d in range(4):
            for e in (1, 2, 3):
                landed(R[chunk].at[pl.ds(0, UNIT)], rb_send.at[chunk, d * 4 + e])


def mixture(rows, hidden, table, gate_s, up_s, down_s, gate_w, up_w, down_w):
    line = np.arange(GROUP)
    a, r = line // UNIT, line % UNIT
    source = ((r % 40) // CAP) * UNIT + (r // 40) * 40 + a * CAP + r % CAP
    swap = jnp.asarray(source[:, None] == line[None, :], jnp.bfloat16)
    dma = pltpu.SemaphoreType.DMA
    width, inner = gate_w.shape

    def each(shape):
        return [pltpu.VMEM(shape + (size,), jnp.bfloat16) for _, size in CUTS]

    vmem = pl.BlockSpec(memory_space=pltpu.VMEM)
    hbm = pl.BlockSpec(memory_space=pl.ANY)
    return pl.pallas_call(
        mixture_kernel,
        out_shape=jax.ShapeDtypeStruct(rows.shape, jnp.bfloat16),
        in_specs=[vmem] * 7 + [hbm] * 3,
        out_specs=vmem,
        scratch_shapes=[
            pltpu.VMEM((width, inner), jnp.bfloat16),
            pltpu.VMEM((width, inner), jnp.bfloat16),
            pltpu.VMEM((inner, width), jnp.bfloat16),
            pltpu.VMEM((3, 8, 16, BLOCK), jnp.float32),
            *each((8 * BLOCK,)),
            *each((4, GROUP)),
            *each((4, GROUP)),
            *each((4, GROUP)),
            *each((4, GROUP)),
            *each((4 * GROUP,)),
            *[pltpu.VMEM((4 * GROUP, 8 * BLOCK), jnp.bfloat16) for _ in CUTS],
            *each((4 * BLOCK,)),
            *each((3, BLOCK)),
            dma((3,)),
            dma((3, 4)),
            dma((3, 8)),
            dma((3, 4)),
            dma((3, 4)),
            dma((3, 8)),
            dma((3, 4)),
            dma((3, 4)),
            dma((3, 4)),
            dma((3, 16)),
            dma((3, 16)),
            dma((3, 16)),
            dma((3, 16)),
            dma((3, 16)),
            dma((3, 16)),
            dma((3,)),
            dma((3,)),
            dma((3, 3)),
            dma((3, 3)),
        ],
        compiler_params=pltpu.CompilerParams(
            collective_id=1, has_side_effects=True, vmem_limit_bytes=64000000
        ),
        cost_estimate=pl.CostEstimate(flops=25 * 10**9, bytes_accessed=12 * 10**6, transcendentals=0),
        name="mixture",
    )(rows, hidden, table, swap, gate_s, up_s, down_s, gate_w, up_w, down_w)


def shards(
    states,
    input_gain,
    query_weight,
    key_weight,
    value_weight,
    query_gain,
    key_gain,
    output_weight,
    mixture_gain,
    expert_gate,
    expert_up,
    expert_down,
    gate_scale,
    up_scale,
    down_scale,
    expert_index,
    expert_slot,
    route_weight,
):
    pair_count, length, features = states.shape
    context = attend(
        states, input_gain, query_weight, key_weight, value_weight, query_gain, key_gain
    )
    head_width = context.shape[2]
    tp_count = lax.axis_size("tp")
    block_rows = length // tp_count
    ordered = jnp.transpose(context, (1, 0, 2)).reshape(length * pair_count, head_width)
    own_rows = lax.psum_scatter(
        jnp.dot(ordered, output_weight, preferred_element_type=jnp.float32).astype(jnp.bfloat16),
        "tp",
        scatter_dimension=0,
        tiled=True,
    ).astype(jnp.float32)
    own_states = lax.dynamic_slice_in_dim(states, lax.axis_index("tp") * block_rows, block_rows, 1)
    hidden_state = own_states.astype(jnp.float32) + jnp.transpose(
        own_rows.reshape(block_rows, pair_count, features), (1, 0, 2)
    )
    expert_input = rms_scale(hidden_state, mixture_gain).astype(jnp.bfloat16)
    columns = (expert_index[0] * CAP + expert_slot[0]).astype(jnp.float32)
    table = jnp.concatenate([columns.T, route_weight[0].T], axis=0)
    result = mixture(
        expert_input[0],
        hidden_state[0],
        table,
        gate_scale,
        up_scale,
        down_scale,
        expert_gate[0],
        expert_up[0],
        expert_down[0],
    )
    return result[None]


def solution(mesh):
    return jax.shard_map(
        shards,
        mesh=mesh,
        in_specs=(
            P(("batch", "ep"), None, None),
            P(),
            P(None, "tp"),
            P(None, "tp"),
            P(None, "tp"),
            P(),
            P(),
            P("tp", None),
            P(),
            P(("batch", "tp", "ep"), None, None),
            P(("batch", "tp", "ep"), None, None),
            P(("batch", "tp", "ep"), None, None),
            P(("batch", "tp", "ep"), None),
            P(("batch", "tp", "ep"), None),
            P(("batch", "tp", "ep"), None),
            P(("batch", "ep"), "tp", None),
            P(("batch", "ep"), "tp", None),
            P(("batch", "ep"), "tp", None),
        ),
        out_specs=P(("batch", "ep"), "tp", None),
        check_vma=False,
    )
```

profile of v0, /device:TPU:1, one launch (start us, length us, event | category | flops | bytes accessed | tf_op | source)
XLA Modules:
  0.0 239.2 jit_solution(11366139156644856386)
XLA Ops:
  6.5 0.0 copy-start
  6.5 0.0 copy-start.1
  6.5 0.0 reduce-scatter.2.cloned.1.call-start
  6.6 2.2 fusion.1
  8.8 0.0 copy-done.1
  8.8 4.6 %convolution_bitcast_fusion = f32[64,8,8,128]{3,1,2,0:T(8,128)S(1)} fusion(bf16[2048,1024]{1,0:T(8,128)(2,1)} %param.21, bf16[1,512,2048]{2,1,0:T(8,128)(2,1)S(1)} %copy-done.1, f32[2048]{0:T(1024)} %param.20, f32[512]{0:T(512)S(1)} %add_rsqrt_fusion.2), kind=kOutput, calls=%fused_computation.19 | convolution fusion | flops 2151677952 | bytes 8398848 | tf_op jit(solution)/shard_map/dot_general | solution.py:44
  13.4 0.5 copy.37
  13.9 0.0 copy-start.9
  13.9 0.0 copy-start.10
  13.9 0.6 multiply_reduce_fusion
  14.5 0.1 copy.27
  14.6 1.0 fusion.23
  15.6 0.0 copy-done.9
  15.6 0.0 copy-done.10
  15.6 0.0 copy-start.7
  15.7 0.0 copy-start.8
  15.7 2.5 %multiply_reduce_fusion.2 = (f32[512]{0:T(512)S(1)}, f32[512,128]{0,1:T(8,128)S(1)}) fusion(bf16[2048,128]{1,0:T(8,128)(2,1)S(1)} %copy-done.9, bf16[1,512,2048]{2,1,0:T(8,128)(2,1)} %param.19, f32[2048]{0:T(1024)S(1)} %copy-done.10, f32[512]{0:T(512)S(1)} %add_rsqrt_fusion.2), kind=kOutput, calls=%fused_computation.38 | convolution fusion | flops 272760320 | bytes 2895872 | tf_op jit(solution)/shard_map/dot_general | solution.py:48
  18.2 0.0 copy-done.7
  18.2 0.1 multiply_bitcast_fusion
  18.3 0.6 fusion.28
  18.9 0.0 copy-done.8
  18.9 0.6 fusion.9
  19.5 0.8 fusion.14
  20.3 0.0 copy-start.2
  20.3 5.2 %bitcast_reduce_fusion = (f32[8,512]{1,0:T(8,128)S(1)}, f32[512,512,8]{1,0,2:T(8,128)}) fusion(bf16[512,8,64]{2,0,1:T(8,128)(2,1)S(1)} %get-tuple-element.8, bf16[512,8,64]{2,0,1:T(8,128)(2,1)S(1)} %get-tuple-element.7, bf16[512,64]{0,1:T(8,128)(2,1)S(1)} %get-tuple-element.10, bf16[512,64]{0,1:T(8,128)(2,1)S(1)} %get-tuple-element.9), kind=kOutput, calls=%fused_computation.1 | convolution fusion | flops 543420416 | bytes 9584640 | tf_op jit(solution)/shard_map/pshgd,pthd->phgst/dot_general | solution.py:60
  25.5 0.0 copy-done
  25.5 0.0 copy-done.2
  25.5 7.0 %fusion.10 = bf16[128,8,512]{2,0,1:T(8,128)(2,1)} fusion(f32[8,512]{1,0:T(8,128)S(1)} %get-tuple-element.15, f32[512,512,8]{1,0,2:T(8,128)} %get-tuple-element.16, bf16[2048,128]{1,0:T(8,128)(2,1)S(1)} %copy-done, bf16[1,512,2048]{2,1,0:T(8,128)(2,1)S(1)} %copy-done.2, f32[2048]{0:T(1024)S(1)} %copy-done.10, f32[512]{0:T(512)S(1)} %add_rsqrt_fusion.2), kind=kOutput, calls=%fused_computation.20 | convolution fusion | flops 816381952 | bytes 12085248 | tf_op jit(solution)/shard_map/phgst,pthd->pshgd/dot_general | solution.py:65
  32.6 6.4 %convolution_convert_fusion = bf16[512,2048]{1,0:T(8,128)(2,1)} fusion(bf16[512,1024]{0,1:T(8,128)(2,1)} %bitcast.87, bf16[1024,2048]{1,0:T(8,128)(2,1)} %param.26), kind=kOutput, calls=%fused_computation.12 | convolution fusion | flops 2148532224 | bytes 7340032 | tf_op jit(solution)/shard_map/dot_general | solution.py:612
  39.0 0.0 copy-start.4
  39.0 0.0 copy-start.5
  39.0 0.0 copy-start.6
  39.0 0.0 copy-start.3
  39.0 0.0 reduce-scatter.2.cloned.1.call-update
  39.0 0.6 copy-done.4
  39.7 0.0 copy-done.5
  39.7 0.0 copy-done.6
  39.7 0.6 pad_maximum_fusion.table_ref
  40.3 32.0 %reduce-scatter.2.cloned.1.call-done = bf16[128,2048]{1,0:T(8,128)(2,1)} async-done(((bf16[512,2048]{1,0:T(8,128)(2,1)}), bf16[128,2048]{1,0:T(8,128)(2,1)}) %reduce-scatter.2.cloned.1.call-update) | async-done | bytes 524304 | tf_op jit(solution)/shard_map/reduce_scatter | solution.py:611
  72.4 1.3 multiply_reduce_fusion.1
  73.7 0.0 copy-done.3
  73.7 2.4 %fusion.20 = (f32[128,2048]{1,0:T(8,128)}, bf16[128,2048]{1,0:T(8,128)(2,1)}) fusion(bf16[128,2048]{1,0:T(8,128)(2,1)} %reduce-scatter.2.cloned.1.call-done, bf16[1,512,2048]{2,1,0:T(8,128)(2,1)S(1)} %copy-done.2, s32[]{:T(128)S(6)} %select_n.3, f32[2048]{0:T(1024)S(1)} %copy-done.3, f32[128]{0:T(128)S(1)} %add_rsqrt_fusion.3), kind=kLoop, calls=%fused_computation.32 | loop fusion | flops 1572864 | bytes 2630148 | tf_op jit(solution)/shard_map/squeeze | solution.py:626
  76.1 154.4 %mixture.1 = bf16[128,2048]{1,0:T(8,128)(2,1)} custom-call(bf16[128,2048]{1,0:T(8,128)(2,1)} %get-tuple-element.6.rows_ref, f32[128,2048]{1,0:T(8,128)} %get-tuple-element.5.hidden_ref, f32[16,128]{1,0:T(8,128)} %pad_maximum_fusion.table_ref, bf16[320,320]{1,0:T(8,128)(2,1)} %constant.41.clone.swap_ref, f32[1,768]{1,0:T(1,128)} %gate_scale.1, ...), custom_call_target="tpu_custom_call" | custom-call | flops 24999999488 | bytes 12000000 | tf_op jit(solution)/shard_map/mixture/pallas_call | solution.py:536
  230.5 1.9 copy.42
  (6 shorter events, 0.1 us)
Async XLA Ops:
  6.5 19.0 %copy-start = (bf16[2048,128]{1,0:T(8,128)(2,1)S(1)}, bf16[2048,128]{1,0:T(8,128)(2,1)}, u32[]{:S(2)}) copy-start(bf16[2048,128]{1,0:T(8,128)(2,1)} %param.23) | copy-start | bytes 1572868
  6.5 2.3 copy-start.1
  6.5 65.8 %reduce-scatter.2.cloned.1.call-start = ((), (), s32[]{:S(2)}) async-start(), calls=%async_computation.1 | async-start | bytes 2621440 | tf_op jit(solution)/shard_map/reduce_scatter | solution.py:611
  13.9 1.7 copy-start.9
  13.9 1.7 copy-start.10
  15.6 2.6 %copy-start.7 = (f32[128]{0:T(128)S(1)}, f32[128]{0:T(128)}, u32[]{:S(2)}) copy-start(f32[128]{0:T(128)} %param.25) | copy-start | bytes 1540
  15.7 3.2 %copy-start.8 = (f32[128]{0:T(128)S(1)}, f32[128]{0:T(128)}, u32[]{:S(2)}) copy-start(f32[128]{0:T(128)} %param.24) | copy-start | bytes 1540
  20.3 5.2 %copy-start.2 = (bf16[1,512,2048]{2,1,0:T(8,128)(2,1)S(1)}, bf16[1,512,2048]{2,1,0:T(8,128)(2,1)}, u32[]{:S(2)}) copy-start(bf16[1,512,2048]{2,1,0:T(8,128)(2,1)} %param.19) | copy-start | bytes 6291460
  39.0 0.7 copy-start.4
  39.0 0.7 copy-start.5
  39.0 0.7 copy-start.6
  39.0 34.7 %copy-start.3 = (f32[2048]{0:T(1024)S(1)}, f32[2048]{0:T(1024)}, u32[]{:S(2)}) copy-start(f32[2048]{0:T(1024)} %param.27) | copy-start | bytes 24580
Sparse Core Ops, SparseCore 0:
  39.2 33.1 reduce-scatter.1
where the time goes:
time: 240 us; the launch traced here: 239 us
  Pallas kernels  154 us (64%)
  waiting for transfers between devices  32.1 us (13%)
  matrix products  25.8 us (11%)
  between operations  13.6 us (6%)
  other arithmetic  10.2 us (4%)
  local copies, waits for them, and re-layouts  3.18 us (1%)
    pallas_call x1, Pallas kernels, mixture(): pl.pallas_call(mixture_kernel, out_shape=jax.ShapeDtypeStruct(rows.shape,...  154 us
    reduce_scatter x1, waiting for transfers between devices, shards(): lax.psum_scatter(jnp.dot(ordered, output_weight, preferred_element_type=j...  32 us
    dot_general x1, matrix products, attend(): jnp.einsum('phgst,pthd->pshgd', probabilities, value_vectors, preferred_e...  7.04 us
    dot_general x1, matrix products, shards(): jnp.dot(ordered, output_weight, preferred_element_type=jnp.float32)  6.43 us
    dot_general x1, matrix products, attend(): jnp.einsum('pshgd,pthd->phgst', queries, key_vectors, preferred_element_t...  5.21 us
  transfers between devices with their start and end apart: 1, of which 1 were waited for; matrix products, arithmetic and copies ran while one was open for 0% of the time, Pallas kernels for 0%

commit v1 on v0

--- a/solution.py
+++ b/solution.py
@@ -7,66 +7,6 @@
 from jax.experimental import pallas as pl
 from jax.experimental.pallas import tpu as pltpu
 from jax.sharding import PartitionSpec as P
-
-
-def rms_scale(values, scaling):
-    mean_square = jnp.mean(values * values, axis=-1, keepdims=True)
-    return values * lax.rsqrt(mean_square + 1e-06) * scaling
-
-
-def rotate(values, positions):
-    half_dim = values.shape[-1] // 2
-    freq_index = jnp.arange(half_dim, dtype=jnp.float32)
-    frequency = jnp.exp(-(2.0 * freq_index / values.shape[-1]) * math.log(1000000.0))
-    angles = positions[:, None] * frequency[None, :]
-    cosine_table = jnp.cos(angles)[:, None, :]
-    sine_table = jnp.sin(angles)[:, None, :]
-    first_half = values[..., :half_dim]
-    second = values[..., half_dim:]
-    return jnp.concatenate(
-        [
-            first_half * cosine_table - second * sine_table,
-            second * cosine_table + first_half * sine_table,
-        ],
-        axis=-1,
-    )
-
-
-def attend(pair_states, input_gain, query_weight, key_weight, value_weight, query_gain, key_gain):
-    pair_count, length, features = pair_states.shape
-    head_size = query_gain.shape[0]
-    normed = (
-        rms_scale(pair_states.astype(jnp.float32), input_gain)
-        .astype(jnp.bfloat16)
-        .reshape(pair_count * length, features)
-    )
-    positions = jnp.arange(length, dtype=jnp.float32)
-    queries = jnp.dot(normed, query_weight, preferred_element_type=jnp.float32).reshape(
-        pair_count, length, -1, head_size
-    )
-    queries = rotate(rms_scale(queries, query_gain), positions).astype(jnp.bfloat16)
-    key_vectors = jnp.dot(normed, key_weight, preferred_element_type=jnp.float32).reshape(
-        pair_count, length, -1, head_size
-    )
-    key_vectors = rotate(rms_scale(key_vectors, key_gain), positions).astype(jnp.bfloat16)
-    value_vectors = (
-        jnp.dot(normed, value_weight, preferred_element_type=jnp.float32)
-        .astype(jnp.bfloat16)
-        .reshape(pair_count, length, -1, head_size)
-    )
-    kv_count = key_vectors.shape[2]
-    group_size = queries.shape[2] // kv_count
-    queries = queries.reshape(pair_count, length, kv_count, group_size, head_size)
-    scores = jnp.einsum(
-        "pshgd,pthd->phgst", queries, key_vectors, preferred_element_type=jnp.float32
-    ) * (1.0 / math.sqrt(head_size))
-    weights = jnp.exp(scores)
-    probabilities = (weights / jnp.sum(weights, axis=-1, keepdims=True)).astype(jnp.bfloat16)
-    context = jnp.einsum(
-        "phgst,pthd->pshgd", probabilities, value_vectors, preferred_element_type=jnp.float32
-    )
-    return context.astype(jnp.bfloat16).reshape(pair_count, length, -1)
-
 
 MESH = pl.DeviceIdType.MESH
 CUTS = ((0, 768), (768, 640), (1408, 640))
@@ -580,6 +520,241 @@
     )(rows, hidden, table, swap, gate_s, up_s, down_s, gate_w, up_w, down_w)
 
 
+EPS = 1e-06
+SEQ = 512
+HEAD = 128
+
+
+def attention_kernel(
+    states_hbm,
+    input_gain,
+    query_gain,
+    key_gain,
+    cosine,
+    sine,
+    mixture_gain,
+    query_hbm,
+    key_hbm,
+    value_hbm,
+    output_hbm,
+    rows_out,
+    hidden_out,
+    states,
+    normed,
+    query_w,
+    kv_w,
+    output_w,
+    queries,
+    keys,
+    values,
+    context,
+    leaving,
+    halves,
+    arrived,
+    load_sem,
+    half_send,
+    half_recv,
+    full_send,
+    full_recv,
+):
+    me = position()
+    z = me["z"]
+    width = states.shape[1]
+    half = width // 2
+    heads = query_w.shape[1] // HEAD
+    ahead = moved(me, "z", step(z, 1))
+    behind = moved(me, "z", step(z, 3))
+    barrier = pltpu.get_barrier_semaphore()
+    for neighbour in (ahead, behind):
+        pl.semaphore_signal(barrier, inc=1, device_id=neighbour, device_id_type=MESH)
+
+    loads = [
+        pltpu.make_async_copy(src, dst, load_sem.at[n])
+        for n, (src, dst) in enumerate(
+            (
+                (states_hbm, states),
+                (key_hbm, kv_w.at[:, pl.ds(0, HEAD)]),
+                (value_hbm, kv_w.at[:, pl.ds(HEAD, HEAD)]),
+                (query_hbm, query_w),
+                (output_hbm, output_w),
+            )
+        )
+    ]
+    for load in loads:
+        load.start()
+
+    loads[0].wait()
+
+    def norm(i, carry):
+        part = states[rows_at(i, 128), :].astype(jnp.float32)
+        scale = lax.rsqrt(jnp.mean(part * part, axis=-1, keepdims=True) + EPS)
+        normed[rows_at(i, 128), :] = (part * scale * input_gain[...]).astype(jnp.bfloat16)
+        return carry
+
+    lax.fori_loop(0, SEQ // 128, norm, 0)
+
+    def turn(part, gain, factor):
+        scale = lax.rsqrt(jnp.mean(part * part, axis=-1, keepdims=True) + EPS) * factor
+        part = part * gain
+        return (
+            (part * cosine[...] + pltpu.roll(part, HEAD // 2, 1) * sine[...]) * scale
+        ).astype(jnp.bfloat16)
+
+    loads[1].wait()
+    loads[2].wait()
+    both = jnp.dot(normed[...], kv_w[...], preferred_element_type=jnp.float32)
+    keys[...] = turn(both[:, :HEAD], key_gain[...], 1.0)
+    values[:, :HEAD] = both[:, HEAD:].astype(jnp.bfloat16)
+    values[:, HEAD:] = jnp.ones((SEQ, HEAD), jnp.bfloat16)
+    loads[3].wait()
+    factor = math.log2(math.e) / math.sqrt(HEAD)
+
+    def project(n, carry):
+        pair = jnp.dot(
+            normed[...], query_w[:, rows_at(n, 2 * HEAD)], preferred_element_type=jnp.float32
+        )
+        for h in range(2):
+            head = turn(pair[:, h * HEAD : (h + 1) * HEAD], query_gain[...], factor)
+            for i in range(4):
+                queries[i, rows_at(2 * n + h, BLOCK), :] = head[i * BLOCK : (i + 1) * BLOCK]
+        return carry
+
+    lax.fori_loop(0, heads // 2, project, 0)
+    loads[4].wait()
+    pl.semaphore_wait(barrier, 2)
+
+    def block(index):
+        for n in range(heads // 2):
+            scores = lax.dot_general(
+                queries[index, n * 2 * BLOCK : (n + 1) * 2 * BLOCK, :],
+                keys[...],
+                (((1,), (1,)), ((), ())),
+                preferred_element_type=jnp.float32,
+            )
+            mixed = jnp.dot(
+                jnp.exp2(scores).astype(jnp.bfloat16),
+                values[...],
+                preferred_element_type=jnp.float32,
+            )
+            mixed = (mixed[:, :HEAD] / mixed[:, HEAD:]).astype(jnp.bfloat16)
+            for h in range(2):
+                context[:, (2 * n + h) * HEAD : (2 * n + h + 1) * HEAD] = mixed[
+                    h * BLOCK : (h + 1) * BLOCK
+                ]
+
+    def part(side):
+        return jnp.dot(
+            context[...],
+            output_w[:, side * half : (side + 1) * half],
+            preferred_element_type=jnp.float32,
+        )
+
+    block(step(z, 2))
+    for side, device in ((0, ahead), (1, behind)):
+        leaving[2, side] = part(side).astype(jnp.bfloat16)
+        push(
+            leaving.at[2, side], halves.at[side], half_send.at[side], half_recv.at[side], device
+        )
+    for way, (distance, device) in enumerate(((1, ahead), (3, behind))):
+        block(step(z, distance))
+        for side in (1 - way, way):
+            total = part(side)
+            if side == way:
+                landed(halves.at[side], half_recv.at[side])
+                total = total + halves[side].astype(jnp.float32)
+            leaving[way, side] = total.astype(jnp.bfloat16)
+            push(
+                leaving.at[way, side],
+                arrived.at[way, side],
+                full_send.at[way, side],
+                full_recv.at[way, side],
+                device,
+            )
+    block(z)
+    for side in range(2):
+        columns = slice(side * half, (side + 1) * half)
+        hidden_out[:, columns] = part(side) + states[rows_at(z, BLOCK), columns].astype(
+            jnp.float32
+        )
+    for side in range(2):
+        columns = slice(side * half, (side + 1) * half)
+        for way in range(2):
+            landed(arrived.at[way, side], full_recv.at[way, side])
+        hidden_out[:, columns] = hidden_out[:, columns] + (
+            arrived[0, side].astype(jnp.float32) + arrived[1, side].astype(jnp.float32)
+        )
+    hidden = hidden_out[...]
+    scale = lax.rsqrt(jnp.mean(hidden * hidden, axis=-1, keepdims=True) + EPS)
+    rows_out[...] = (hidden * scale * mixture_gain[...]).astype(jnp.bfloat16)
+    for side in range(2):
+        landed(halves.at[side], half_send.at[side])
+        for way in range(2):
+            landed(arrived.at[way, side], full_send.at[way, side])
+
+
+def attention(
+    states, input_gain, query_w, key_w, value_w, query_gain, key_gain, output_w, mixture_gain
+):
+    length, width = states.shape
+    span = query_w.shape[1]
+    index = np.arange(HEAD // 2, dtype=np.float64)
+    angles = np.arange(length, dtype=np.float64)[:, None] * 1e6 ** (-2.0 * index / HEAD)[None, :]
+    cosine = np.concatenate([np.cos(angles)] * 2, axis=1).astype(np.float32)
+    sine = np.concatenate([-np.sin(angles), np.sin(angles)], axis=1).astype(np.float32)
+    vmem = pl.BlockSpec(memory_space=pltpu.VMEM)
+    hbm = pl.BlockSpec(memory_space=pl.ANY)
+    dma = pltpu.SemaphoreType.DMA
+    half = width // 2
+    bf16 = jnp.bfloat16
+    return pl.pallas_call(
+        attention_kernel,
+        out_shape=(
+            jax.ShapeDtypeStruct((BLOCK, width), bf16),
+            jax.ShapeDtypeStruct((BLOCK, width), jnp.float32),
+        ),
+        in_specs=[hbm] + [vmem] * 6 + [hbm] * 4,
+        out_specs=(vmem, vmem),
+        scratch_shapes=[
+            pltpu.VMEM((length, width), bf16),
+            pltpu.VMEM((length, width), bf16),
+            pltpu.VMEM((width, span), bf16),
+            pltpu.VMEM((width, 2 * HEAD), bf16),
+            pltpu.VMEM((span, width), bf16),
+            pltpu.VMEM((4, span, HEAD), bf16),
+            pltpu.VMEM((length, HEAD), bf16),
+            pltpu.VMEM((length, 2 * HEAD), bf16),
+            pltpu.VMEM((BLOCK, span), bf16),
+            pltpu.VMEM((3, 2, BLOCK, half), bf16),
+            pltpu.VMEM((2, BLOCK, half), bf16),
+            pltpu.VMEM((2, 2, BLOCK, half), bf16),
+            dma((5,)),
+            dma((2,)),
+            dma((2,)),
+            dma((2, 2)),
+            dma((2, 2)),
+        ],
+        compiler_params=pltpu.CompilerParams(
+            collective_id=2, has_side_effects=True, vmem_limit_bytes=48000000
+        ),
+        cost_estimate=pl.CostEstimate(
+            flops=6 * 10**9, bytes_accessed=13 * 10**6, transcendentals=2 * 10**6
+        ),
+        name="attention",
+    )(
+        states,
+        input_gain[None],
+        query_gain[None],
+        key_gain[None],
+        jnp.asarray(cosine),
+        jnp.asarray(sine),
+        mixture_gain[None],
+        query_w,
+        key_w,
+        value_w,
+        output_w,
+    )
+
+
 def shards(
     states,
     input_gain,
@@ -600,30 +775,22 @@
     expert_slot,
     route_weight,
 ):
-    pair_count, length, features = states.shape
-    context = attend(
-        states, input_gain, query_weight, key_weight, value_weight, query_gain, key_gain
+    rows, hidden = attention(
+        states[0],
+        input_gain,
+        query_weight,
+        key_weight,
+        value_weight,
+        query_gain,
+        key_gain,
+        output_weight,
+        mixture_gain,
     )
-    head_width = context.shape[2]
-    tp_count = lax.axis_size("tp")
-    block_rows = length // tp_count
-    ordered = jnp.transpose(context, (1, 0, 2)).reshape(length * pair_count, head_width)
-    own_rows = lax.psum_scatter(
-        jnp.dot(ordered, output_weight, preferred_element_type=jnp.float32).astype(jnp.bfloat16),
-        "tp",
-        scatter_dimension=0,
-        tiled=True,
-    ).astype(jnp.float32)
-    own_states = lax.dynamic_slice_in_dim(states, lax.axis_index("tp") * block_rows, block_rows, 1)
-    hidden_state = own_states.astype(jnp.float32) + jnp.transpose(
-        own_rows.reshape(block_rows, pair_count, features), (1, 0, 2)
-    )
-    expert_input = rms_scale(hidden_state, mixture_gain).astype(jnp.bfloat16)
     columns = (expert_index[0] * CAP + expert_slot[0]).astype(jnp.float32)
     table = jnp.concatenate([columns.T, route_weight[0].T], axis=0)
     result = mixture(
-        expert_input[0],
-        hidden_state[0],
+        rows,
+        hidden,
         table,
         gate_scale,
         up_scale,

time: 240 us -> 209 us (0.87)
  Pallas kernels: 154 us -> 195 us
  waiting for transfers between devices: 32.1 us -> 0 us
  matrix products: 25.8 us -> 0 us
  between operations: 13.6 us -> 0.04 us
  local copies, waits for them, and re-layouts: 3.18 us -> 11.9 us
  other arithmetic: 10.2 us -> 1.99 us
    pallas_call x0 -> x1, Pallas kernels: none -> 36.1 us  [attention(): pl.pallas_call(attention_kernel, out_shape=(jax.ShapeDtypeStruct((BLOCK,...]
    reduce_scatter x1 -> x0, waiting for transfers between devices: 32 us -> none  [shards(): lax.psum_scatter(jnp.dot(ordered, output_weight, preferred_element_type=j...]
    dot_general x5 -> x0, matrix products: 25.8 us -> none  [the longest x1 7.04 us: attend(): jnp.einsum('phgst,pthd->pshgd', probabilities, value_vectors, preferred_e...]
    unnamed x24 -> x23, local copies, waits for them, and re-layouts: 3.09 us -> 11.9 us
    pallas_call x1, Pallas kernels: 154 us -> 159 us  [mixture(): pl.pallas_call(mixture_kernel, out_shape=jax.ShapeDtypeStruct(rows.shape,...]
    reduce_sum x3 -> x0, other arithmetic: 4.13 us -> none  [rms_scale(): mean_square = jnp.mean(values * values, axis=-1, keepdims=True)]
    squeeze x1 -> x0, other arithmetic: 2.41 us -> none  [shards(): hidden_state[0]]
  transfers between devices with their start and end apart: 1 -> 0, of which waited for: 1 -> 0; matrix products, arithmetic and copies ran while one was open for 0% -> 0% of each run, Pallas kernels for 0% -> 0%
where the time goes in v1:
time: 209 us
  Pallas kernels  195 us (93%)
  local copies, waits for them, and re-layouts  11.9 us (6%)
    pallas_call x1, Pallas kernels, mixture(): pl.pallas_call(mixture_kernel, out_shape=jax.ShapeDtypeStruct(rows.shape,...  159 us
    pallas_call x1, Pallas kernels, attention(): pl.pallas_call(attention_kernel, out_shape=(jax.ShapeDtypeStruct((BLOCK,...  36.1 us
    unnamed x23, local copies, waits for them, and re-layouts  11.9 us

profile of v1, /device:TPU:1, one launch (start us, length us, event | category | flops | bytes accessed | tf_op | source)
XLA Modules:
  0.0 208.6 jit_solution(13979927761035513561)
XLA Ops:
  0.0 0.7 convert_bitcast_fusion
  0.7 1.3 pad_maximum_fusion.table_ref
  2.0 0.0 copy-start
  2.0 1.6 copy-done
  3.6 0.0 copy-start.1
  3.6 1.0 copy-done.1
  4.6 0.0 copy-start.2
  4.6 1.0 copy-done.2
  5.7 0.0 copy-start.3
  5.7 0.7 copy-done.3
  6.4 0.0 copy-start.4
  6.4 0.7 copy-done.4
  7.1 0.0 copy-start.5
  7.1 0.7 copy-done.5
  7.7 0.0 copy-start.6
  7.7 0.7 copy-done.6
  8.4 0.0 copy-start.7
  8.4 0.9 copy-done.7
  9.3 0.0 copy-start.8
  9.3 0.9 copy-done.8
  10.3 36.1 %attention.1 = (bf16[128,2048]{1,0:T(8,128)(2,1)S(1)}, f32[128,2048]{1,0:T(8,128)S(1)}) custom-call(bf16[512,2048]{1,0:T(8,128)(2,1)S(1)} %bitcast.16, f32[1,2048]{1,0:T(1,128)S(1)} %bitcast.17, f32[1,128]{1,0:T(1,128)S(1)} %bitcast.19, f32[1,128]{1,0:T(1,128)S(1)} %bitcast.20, f32[512,128]{1,0:T(8,128)S(1)} %copy-done.8, f32[512,128]{1,0:T(8,128)S(1)} %copy-done.7, ...), custom_call_target="tpu_custom_call" | custom-call | flops 6000000000 | bytes 13000000 | tf_op jit(solution)/shard_map/attention/pallas_call | solution.py:709
  46.4 0.0 copy-start.9
  46.4 1.0 copy-done.9
  47.4 0.0 copy-start.10
  47.4 0.8 copy-done.10
  48.2 158.6 %mixture.1 = bf16[128,2048]{1,0:T(8,128)(2,1)} custom-call(bf16[128,2048]{1,0:T(8,128)(2,1)} %copy-done.10, f32[128,2048]{1,0:T(8,128)} %copy-done.9, f32[16,128]{1,0:T(8,128)} %pad_maximum_fusion.table_ref, bf16[320,320]{1,0:T(8,128)(2,1)} %constant.10.clone.swap_ref, f32[1,768]{1,0:T(1,128)} %gate_scale.1, f32[1,768]{1,0:T(1,128)} %up_scale.1, ...), custom_call_target="tpu_custom_call" | custom-call | flops 24999999488 | bytes 12000000 | tf_op jit(solution)/shard_map/mixture/pallas_call | solution.py:476
  206.8 1.9 copy.23
Async XLA Ops:
  2.0 1.6 copy-start
  3.6 1.0 copy-start.1
  4.6 1.0 copy-start.2
  5.7 0.7 copy-start.3
  6.4 0.7 copy-start.4
  7.1 0.7 copy-start.5
  7.7 0.7 copy-start.6
  8.4 0.9 copy-start.7
  9.3 0.9 copy-start.8
  46.4 1.0 copy-start.9
  47.4 0.8 copy-start.10
